TPU v7x, 32 devices: a whole 2x2x4 slice. The times are simulated.
32 devices in a mesh: fsdp: 4 (over z), ctx: 4 (over y, core), tp: 2 (over x).
Axes of the slice: x: 2, y: 2, z: 4, core: 2. Of those that a mesh axis runs over, the one named last changes fastest.
Arguments:
- block_input: bfloat16 [4, 1024, 1024], P('fsdp', 'ctx'), may hold values from -6 to 6
- input_gain: float32 [1024], replicated, may hold values from 0.5 to 1.5
- gate_proj: bfloat16 [1024, 2048], P('fsdp', 'tp'), may hold values from -0.1875 to 0.1875
- x_proj: bfloat16 [1024, 2048], P('fsdp', 'tp'), may hold values from -0.1875 to 0.1875
- bc_proj: bfloat16 [1024, 256], P('fsdp'), may hold values from -0.1875 to 0.1875
- dt_proj: bfloat16 [1024, 32], P('fsdp', 'tp'), may hold values from -0.1875 to 0.1875
- x_conv: float32 [4, 2048], P(None, 'tp'), may hold values from -3 to 3
- bc_conv: float32 [4, 256], replicated, may hold values from -3 to 3
- dt_bias: float32 [32], P('tp'), may hold values from -2 to 1
- a_log: float32 [32], P('tp'), may hold values from -11 to -2
- skip_gain: float32 [32], P('tp'), may hold values from 0.5 to 1.5
- gated_gain: float32 [2048], P('tp'), may hold values from 0.5 to 1.5
- out_proj: bfloat16 [2048, 1024], P('tp', 'fsdp'), may hold values from -0.125 to 0.125
- cotangent: bfloat16 [4, 1024, 1024], P('fsdp', 'ctx'), may hold values from -6 to 6
Outputs:
- block_output: bfloat16 [4, 1024, 1024], P('fsdp', 'ctx')
- input_grad: float32 [4, 1024, 1024], P('fsdp', 'ctx')
- grad_input_gain: float32 [1024], replicated
- grad_gate_proj: float32 [1024, 2048], P('fsdp', 'tp')
- grad_x_proj: float32 [1024, 2048], P('fsdp', 'tp')
- grad_bc_proj: float32 [1024, 256], P('fsdp')
- grad_dt_proj: float32 [1024, 32], P('fsdp', 'tp')
- grad_x_conv: float32 [4, 2048], P(None, 'tp')
- grad_bc_conv: float32 [4, 256], replicated
- grad_dt_bias: float32 [32], P('tp')
- grad_a_log: float32 [32], P('tp')
- grad_skip_gain: float32 [32], P('tp')
- grad_gated_gain: float32 [2048], P('tp')
- grad_out_proj: float32 [2048, 1024], P('tp', 'fsdp')
All inputs are finite; a program needn't handle non-finite values.
Results may differ from a plain program's by a relative error of at most 0.0098.
Values may be sent and summed in bfloat16 or wider, within the bound.
No kernel may reach another device: no remote copies, remote signals or barrier semaphores. Data moves between devices by JAX's collectives and lax.ppermute only.
A program may use at most 128 MiB of HBM per device.

v0:
```python
import jax
import jax.numpy as jnp
from jax import lax
from jax.sharding import PartitionSpec as P

EPSILON = 1e-05
FINE = lax.Precision.HIGHEST


def from_behind(block, axis, distance):
    devices = range(lax.axis_size(axis))
    route = [(i - distance, i) for i in devices if i - distance in devices]
    return lax.ppermute(block, axis, route)


def carried_in(part, axis, combine, identity, reverse):
    count = lax.axis_size(axis)
    place = lax.axis_index(axis)
    ahead = count - 1 - place if reverse else place
    gathered = jax.tree.map(lambda a: lax.all_gather(a, axis), part)
    state = jax.tree.map(lambda a, e: jnp.zeros_like(a) + jnp.asarray(e, a.dtype), part, identity)

    def one(lap, state):
        source = count - 1 - lap if reverse else lap
        return combine(
            state, jax.tree.map(lambda a: lax.dynamic_index_in_dim(a, source, 0, False), gathered)
        )

    return lax.fori_loop(0, ahead, one, state)


def combine_states(earlier, later):
    return (earlier[0] * later[0], earlier[1] * later[0][:, :, None, None] + later[1])


def silu_slope(values):
    sigmoid_value = jax.nn.sigmoid(values)
    return sigmoid_value * (1.0 + values * (1.0 - sigmoid_value))


def block_local(x_heads, b_rows, c_rows, step_size, log_decay):
    cumulative = jnp.cumsum(log_decay, axis=2)
    log_gaps = cumulative[:, :, :, None] - cumulative[:, :, None, :]
    length = log_decay.shape[2]
    causal = jnp.tril(jnp.ones((length, length), jnp.bool_))
    decays = jnp.where(causal, jnp.exp(jnp.where(causal, log_gaps, 0.0)), 0.0)
    scores = jnp.einsum("btn,bsn->bts", c_rows, b_rows, precision=FINE)
    weights = decays * scores[:, None, :, :] * step_size[:, :, None, :]
    within = jnp.einsum("bhts,bshp->bthp", weights, x_heads, precision=FINE)
    tail_decay = jnp.exp(cumulative[:, :, -1:] - cumulative) * step_size
    summary = jnp.einsum("bhs,bshp,bsn->bhpn", tail_decay, x_heads, b_rows, precision=FINE)
    return (within, summary, jnp.exp(cumulative[:, :, -1]))


def block_carry(c_rows, log_decay, state_in):
    cumulative = jnp.cumsum(log_decay, axis=2)
    carried = jnp.einsum("btn,bhpn->bthp", c_rows, state_in, precision=FINE)
    return jnp.exp(cumulative).transpose(0, 2, 1)[:, :, :, None] * carried


def back_product(grad_low, weight):
    return lax.dot_general(
        grad_low, weight, (((1,), (1,)), ((), ())), preferred_element_type=jnp.float32
    )


def on_device(
    block_input,
    input_gain,
    gate_proj,
    x_proj,
    bc_proj,
    dt_proj,
    x_conv,
    bc_conv,
    dt_bias,
    a_log,
    skip_gain,
    gated_gain,
    out_proj,
    cotangent,
):
    seqs_here, length, model_width = block_input.shape
    row_count = seqs_here * length
    inner_here = gate_proj.shape[1]
    heads_here = dt_proj.shape[1]
    head_size = inner_here // heads_here
    state_size = bc_proj.shape[1] // 2
    tap_count = x_conv.shape[0]
    full_inner = inner_here * lax.axis_size("tp")
    full_gate, full_x, full_bc, full_dt, full_out = (
        lax.all_gather(gate_proj, "fsdp", axis=0, tiled=True),
        lax.all_gather(x_proj, "fsdp", axis=0, tiled=True),
        lax.all_gather(bc_proj, "fsdp", axis=0, tiled=True),
        lax.all_gather(dt_proj, "fsdp", axis=0, tiled=True),
        lax.all_gather(out_proj, "fsdp", axis=1, tiled=True),
    )
    residual = block_input.astype(jnp.float32)
    in_scale = lax.rsqrt(jnp.mean(residual * residual, axis=-1, keepdims=True) + EPSILON)
    normed_low = (
        (residual * in_scale * input_gain).astype(jnp.bfloat16).reshape(row_count, model_width)
    )
    gate_input = jnp.dot(normed_low, full_gate, preferred_element_type=jnp.float32).reshape(
        seqs_here, length, inner_here
    )
    x_input = jnp.dot(normed_low, full_x, preferred_element_type=jnp.float32).reshape(
        seqs_here, length, inner_here
    )
    bc_input = jnp.dot(normed_low, full_bc, preferred_element_type=jnp.float32).reshape(
        seqs_here, length, 2 * state_size
    )
    dt_input = jnp.dot(normed_low, full_dt, preferred_element_type=jnp.float32).reshape(
        seqs_here, length, heads_here
    )
    conv_input = jnp.concatenate([x_input, bc_input], axis=-1)
    conv_taps = jnp.concatenate([x_conv, bc_conv], axis=-1)
    edge_rows = from_behind(conv_input[:, length - tap_count + 1 :, :], "ctx", 1)
    padded = jnp.concatenate([edge_rows, conv_input], axis=1)
    conv_out = jnp.zeros_like(conv_input)
    for offset in range(tap_count):
        conv_out = conv_out + conv_taps[offset] * padded[:, offset : offset + length, :]
    activated = jax.nn.silu(conv_out)
    x_heads = activated[:, :, :inner_here].reshape(seqs_here, length, heads_here, head_size)
    b_rows = activated[:, :, inner_here : inner_here + state_size]
    c_rows = activated[:, :, inner_here + state_size :]
    pre_step = dt_input.transpose(0, 2, 1) + dt_bias[None, :, None]
    step_size = jax.nn.softplus(pre_step)
    decay_rates = jnp.exp(a_log)[None, :, None]
    log_decay = -decay_rates * step_size
    (within, summary, total_decay), local_back = jax.vjp(
        block_local, x_heads, b_rows, c_rows, step_size, log_decay
    )
    identity = (jnp.ones_like(total_decay), jnp.zeros_like(summary))
    state_in = carried_in((total_decay, summary), "ctx", combine_states, identity, False)[1]
    carried, carry_back = jax.vjp(block_carry, c_rows, log_decay, state_in)
    mixed_heads = within + carried + skip_gain[None, None, :, None] * x_heads
    mixed_flat = mixed_heads.reshape(seqs_here, length, inner_here)
    gate_act = jax.nn.silu(gate_input)
    gated_rows = mixed_flat * gate_act
    square_sum = lax.psum(jnp.sum(gated_rows * gated_rows, axis=-1), "tp")
    out_scale = lax.rsqrt(square_sum / full_inner + EPSILON)[:, :, None]
    normed_out = (
        (gated_rows * out_scale * gated_gain).astype(jnp.bfloat16).reshape(row_count, inner_here)
    )
    branch_sum = lax.psum(jnp.dot(normed_out, full_out, preferred_element_type=jnp.float32), "tp")
    block_output = (residual + branch_sum.reshape(seqs_here, length, model_width)).astype(
        jnp.bfloat16
    )
    cot_rows = cotangent.reshape(row_count, model_width)
    grad_out_w = lax.dot_general(
        normed_out, cot_rows, (((0,), (0,)), ((), ())), preferred_element_type=jnp.float32
    )
    d_normed_low = back_product(cot_rows, full_out).astype(jnp.bfloat16)
    d_normed_out = d_normed_low.astype(jnp.float32).reshape(seqs_here, length, inner_here)
    grad_gated_gain = jnp.sum(d_normed_out * gated_rows * out_scale, axis=(0, 1))
    cross_sum = lax.psum(jnp.sum(d_normed_out * gated_gain * gated_rows, axis=-1), "tp")
    d_gated = (
        out_scale * gated_gain * d_normed_out
        - gated_rows * (out_scale**3 / full_inner) * cross_sum[:, :, None]
    )
    d_mixed = (d_gated * gate_act).reshape(seqs_here, length, heads_here, head_size)
    d_gate_low = (
        (d_gated * mixed_flat * silu_slope(gate_input))
        .astype(jnp.bfloat16)
        .reshape(row_count, inner_here)
    )
    grad_skip_gain = jnp.sum(d_mixed * x_heads, axis=(0, 1, 3))
    d_c_carry, d_decay_carry, state_grad = carry_back(d_mixed)
    later_grad = carried_in((total_decay, state_grad), "ctx", combine_states, identity, True)[1]
    d_total = jnp.sum(later_grad * state_in, axis=(2, 3))
    d_x_heads, d_b_rows, d_c_rows, d_step, d_log_decay = local_back((d_mixed, later_grad, d_total))
    d_x_heads = d_x_heads + skip_gain[None, None, :, None] * d_mixed
    d_c_rows = d_c_rows + d_c_carry
    d_log_decay = d_log_decay + d_decay_carry
    grad_a_log = jnp.sum(d_log_decay * log_decay, axis=(0, 2))
    d_pre = (d_step - decay_rates * d_log_decay) * jax.nn.sigmoid(pre_step)
    grad_dt_bias = jnp.sum(d_pre, axis=(0, 2))
    d_dt_low = d_pre.transpose(0, 2, 1).astype(jnp.bfloat16).reshape(row_count, heads_here)
    d_activated = jnp.concatenate(
        [d_x_heads.reshape(seqs_here, length, inner_here), d_b_rows, d_c_rows], axis=-1
    )
    d_conv_out = d_activated * silu_slope(conv_out)
    d_padded = jnp.zeros_like(padded)
    tap_grads = []
    for offset in range(tap_count):
        tap_grads.append(jnp.sum(d_conv_out * padded[:, offset : offset + length, :], axis=(0, 1)))
        d_padded = d_padded.at[:, offset : offset + length, :].add(conv_taps[offset] * d_conv_out)
    grad_taps = jnp.stack(tap_grads)
    edge_grad = from_behind(d_padded[:, : tap_count - 1, :], "ctx", -1)
    d_conv_input = d_padded[:, tap_count - 1 :, :] + jnp.pad(
        edge_grad, ((0, 0), (length - tap_count + 1, 0), (0, 0))
    )
    d_x_low = d_conv_input[:, :, :inner_here].astype(jnp.bfloat16).reshape(row_count, inner_here)
    partial_normed = (
        back_product(d_gate_low, full_gate)
        + back_product(d_x_low, full_x)
        + back_product(d_dt_low, full_dt)
    )
    summed_normed, summed_bc, grad_bc_conv = lax.psum(
        (
            partial_normed,
            d_conv_input[:, :, inner_here:].reshape(row_count, 2 * state_size),
            grad_taps[:, inner_here:],
        ),
        "tp",
    )
    d_bc_low = summed_bc.astype(jnp.bfloat16)
    d_normed = (summed_normed + back_product(d_bc_low, full_bc)).reshape(
        seqs_here, length, model_width
    )

    def weight_grad(grad_low):
        return lax.dot_general(
            normed_low, grad_low, (((0,), (0,)), ((), ())), preferred_element_type=jnp.float32
        )

    weight_grads = (
        weight_grad(d_gate_low),
        weight_grad(d_x_low),
        weight_grad(d_bc_low),
        weight_grad(d_dt_low),
        grad_out_w,
    )
    grad_input_gain = jnp.sum(d_normed * residual * in_scale, axis=(0, 1))
    d_scaled = d_normed * input_gain
    input_grad = (
        cotangent.astype(jnp.float32)
        + in_scale * d_scaled
        - residual
        * (in_scale**3 / model_width)
        * jnp.sum(d_scaled * residual, axis=-1, keepdims=True)
    )
    sectioned = (
        lax.psum_scatter(weight_grads[0], "fsdp", scatter_dimension=0, tiled=True),
        lax.psum_scatter(weight_grads[1], "fsdp", scatter_dimension=0, tiled=True),
        lax.psum_scatter(weight_grads[2], "fsdp", scatter_dimension=0, tiled=True),
        lax.psum_scatter(weight_grads[3], "fsdp", scatter_dimension=0, tiled=True),
        lax.psum_scatter(weight_grads[4], "fsdp", scatter_dimension=1, tiled=True),
    )
    owned_rows = (
        lax.psum_scatter(sectioned[0], "ctx", scatter_dimension=0, tiled=True),
        lax.psum_scatter(sectioned[1], "ctx", scatter_dimension=0, tiled=True),
        lax.psum_scatter(sectioned[2], "ctx", scatter_dimension=0, tiled=True),
        lax.psum_scatter(sectioned[3], "ctx", scatter_dimension=0, tiled=True),
        lax.psum_scatter(sectioned[4], "ctx", scatter_dimension=1, tiled=True),
    )
    grad_gate_proj, grad_x_proj, grad_bc_proj, grad_dt_proj, grad_out_proj = (
        lax.all_gather(owned_rows[0], "ctx", axis=0, tiled=True),
        lax.all_gather(owned_rows[1], "ctx", axis=0, tiled=True),
        lax.all_gather(owned_rows[2], "ctx", axis=0, tiled=True),
        lax.all_gather(owned_rows[3], "ctx", axis=0, tiled=True),
        lax.all_gather(owned_rows[4], "ctx", axis=1, tiled=True),
    )
    small_totals = lax.psum(
        (
            grad_input_gain,
            grad_taps[:, :inner_here],
            grad_bc_conv,
            grad_dt_bias,
            grad_a_log,
            grad_skip_gain,
            grad_gated_gain,
        ),
        ("fsdp", "ctx"),
    )
    return (
        block_output,
        input_grad,
        small_totals[0],
        grad_gate_proj,
        grad_x_proj,
        grad_bc_proj,
        grad_dt_proj,
        small_totals[1],
        small_totals[2],
        small_totals[3],
        small_totals[4],
        small_totals[5],
        small_totals[6],
        grad_out_proj,
    )


def solution(mesh):
    in_specs = (
        P("fsdp", "ctx", None),
        P(),
        P("fsdp", "tp"),
        P("fsdp", "tp"),
        P("fsdp", None),
        P("fsdp", "tp"),
        P(None, "tp"),
        P(),
        P("tp"),
        P("tp"),
        P("tp"),
        P("tp"),
        P("tp", "fsdp"),
        P("fsdp", "ctx", None),
    )
    out_specs = (
        P("fsdp", "ctx", None),
        P("fsdp", "ctx", None),
        P(),
        P("fsdp", "tp"),
        P("fsdp", "tp"),
        P("fsdp", None),
        P("fsdp", "tp"),
        P(None, "tp"),
        P(),
        P("tp"),
        P("tp"),
        P("tp"),
        P("tp"),
        P("tp", "fsdp"),
    )
    return jax.shard_map(
        on_device, mesh=mesh, in_specs=in_specs, out_specs=out_specs, check_vma=False
    )
```

profile of v0, /device:TPU:0, one launch (start us, length us, event | category | flops | bytes accessed | tf_op | source)
XLA Modules:
  0.0 786.6 jit_solution(12926951627118034505)
XLA Ops:
  8.0 15.0 %all_gather.50 = bf16[1024,16]{0,1:T(8,128)(2,1)S(1)} all-gather(bf16[256,16]{0,1:T(8,128)(2,1)} %param.31), channel_id=1, replica_groups=mesh['fsdp'=4,'ctx'=4,'tp'=2] {'fsdp'}, dimensions={0}, use_global_device_ids=true | all-gather | bytes 40960 | tf_op jit(solution)/shard_map/all_gather | solution.py:95
  29.3 22.7 %all_gather.49 = bf16[1024,256]{1,0:T(8,128)(2,1)S(1)} all-gather(bf16[256,256]{1,0:T(8,128)(2,1)S(1)} %copy-done.44), channel_id=1, replica_groups=mesh['fsdp'=4,'ctx'=4,'tp'=2] {'fsdp'}, dimensions={0}, use_global_device_ids=true | all-gather | bytes 655360 | tf_op jit(solution)/shard_map/all_gather | solution.py:94
  54.0 12.6 %all-gather.13.cloned.1.call-done = bf16[1024,1024]{1,0:T(8,128)(2,1)} async-done(((bf16[256,1024]{1,0:T(8,128)(2,1)}), bf16[1024,1024]{1,0:T(8,128)(2,1)}) %all-gather.13.cloned.1.call-update) | async-done | bytes 2097168 | tf_op jit(solution)/shard_map/all_gather | solution.py:93
  83.0 7.0 all-gather
  96.4 7.8 all-gather.25.cloned.1.call-done
  106.3 6.0 fusion.36
  114.9 36.8 %all-gather.15.cloned.1.call-done = bf16[1024,1024]{1,0:T(8,128)(2,1)} async-done(((bf16[256,1024]{1,0:T(8,128)(2,1)}), bf16[1024,1024]{1,0:T(8,128)(2,1)}) %all-gather.15.cloned.1.call-update) | async-done | bytes 2097168 | tf_op jit(solution)/shard_map/all_gather | solution.py:92
  160.3 37.8 %all-gather.17.cloned.1.call-done = bf16[1024,1024]{1,0:T(8,128)(2,1)} async-done(((bf16[1024,256]{1,0:T(8,128)(2,1)}), bf16[1024,1024]{1,0:T(8,128)(2,1)}) %all-gather.17.cloned.1.call-update) | async-done | bytes 2097168 | tf_op jit(solution)/shard_map/all_gather | solution.py:96
  202.2 5.4 psum.93
  231.0 8.6 %fusion.8 = (f32[16,256]{1,0:T(8,128)}, f32[16,256]{1,0:T(8,128)}, f32[16,256]{1,0:T(8,128)}, f32[256,256]{1,0:T(8,128)S(1)}) fusion(f32[16,256]{1,0:T(8,128)S(1)} %copy-done.57, f32[256,256]{1,0:T(8,128)} %fusion.92, f32[16,256]{1,0:T(8,128)S(1)} %copy-done.59, pred[256,256]{1,0:T(8,128)(4,1)} %iota_compare_fusion, f32[16,64,256]{2,1,0:T(8,128)} %bitcast.308, ...), kind=kOutput, calls=%fused_computation.20 | convolution fusion | flops 820957184 | bytes 2768896 | tf_op jit(solution)/shard_map/transpose(jvp(bhts,bshp->bthp))/dot_general | solution.py:49
  244.2 6.0 while.31
  300.4 12.9 %all-reduce.11 = (bf16[256,256]{1,0:T(8,128)(2,1)S(1)}, f32[4,256]{1,0:T(4,128)}) all-reduce(f32[256,256]{1,0:T(8,128)S(1)} %slice_bitcast_fusion, f32[4,256]{1,0:T(4,128)S(1)} %pad_maximum_fusion.2), channel_id=1, replica_groups=mesh['fsdp'=4,'ctx'=4,'tp'=2] {'tp'}, use_global_device_ids=true, to_apply=%region_24.25 | all-reduce | flops 66560 | bytes 401408 | tf_op jit(solution)/shard_map/psum | solution.py:199
  318.3 79.6 %reduce-scatter.29.cloned.1.call-done = f32[1024,256]{1,0:T(8,128)} async-done(((f32[1024,1024]{1,0:T(8,128)}), f32[1024,256]{1,0:T(8,128)}) %reduce-scatter.29.cloned.1.call-update) | async-done | bytes 1048592 | tf_op jit(solution)/shard_map/reduce_scatter | solution.py:238
  400.6 77.0 %reduce-scatter.19.cloned.1.call-done = f32[256,1024]{1,0:T(8,128)} async-done(((f32[1024,1024]{1,0:T(8,128)}), f32[256,1024]{1,0:T(8,128)}) %reduce-scatter.19.cloned.1.call-update) | async-done | bytes 1048592 | tf_op jit(solution)/shard_map/reduce_scatter | solution.py:235
  483.5 16.5 %reduce-scatter.27.cloned.1.call-done = f32[256,16]{0,1:T(8,128)} async-done(((f32[1024,16]{0,1:T(8,128)}), f32[256,16]{0,1:T(8,128)}) %reduce-scatter.27.cloned.1.call-update) | async-done | bytes 16400 | tf_op jit(solution)/shard_map/reduce_scatter | solution.py:237
  502.9 25.2 %reduce-scatter.23.cloned.1.call-done = f32[256,256]{1,0:T(8,128)} async-done(((f32[1024,256]{1,0:T(8,128)}), f32[256,256]{1,0:T(8,128)}) %reduce-scatter.23.cloned.1.call-update) | async-done | bytes 262160 | tf_op jit(solution)/shard_map/reduce_scatter | solution.py:236
  528.2 26.2 %reduce-scatter.17.cloned.1.call-done = f32[64,1024]{1,0:T(8,128)} async-done(((f32[256,1024]{1,0:T(8,128)}), f32[64,1024]{1,0:T(8,128)}) %reduce-scatter.17.cloned.1.call-update) | async-done | bytes 262160 | tf_op jit(solution)/shard_map/reduce_scatter | solution.py:241
  554.4 27.2 %reduce-scatter.33.cloned.1.call-done = f32[64,1024]{1,0:T(8,128)} async-done(((f32[256,1024]{1,0:T(8,128)}), f32[64,1024]{1,0:T(8,128)}) %reduce-scatter.33.cloned.1.call-update) | async-done | bytes 262160
  581.7 27.6 %reduce-scatter.21.cloned.1.call-done = f32[64,1024]{1,0:T(8,128)} async-done(((f32[256,1024]{1,0:T(8,128)}), f32[64,1024]{1,0:T(8,128)}) %reduce-scatter.21.cloned.1.call-update) | async-done | bytes 262160 | tf_op jit(solution)/shard_map/reduce_scatter | solution.py:242
  609.5 22.1 %reduce-scatter.31.cloned.1.call-done = f32[64,16]{1,0:T(8,128)} async-done(((f32[256,16]{1,0:T(8,128)}), f32[64,16]{1,0:T(8,128)}) %reduce-scatter.31.cloned.1.call-update) | async-done | bytes 4112
  632.5 5.2 all-gather.3
  638.4 59.9 %all-reduce.10.cloned.1.call-done = (f32[1,256,1024]{2,1,0:T(8,128)}, f32[256,1024]{1,0:T(8,128)}) async-done(((f32[1,256,1024]{2,1,0:T(8,128)}, f32[256,1024]{1,0:T(8,128)}), (f32[1,256,1024]{2,1,0:T(8,128)}, f32[256,1024]{1,0:T(8,128)})) %all-reduce.10.cloned.1.call-update) | async-done | bytes 2097168 | tf_op jit(solution)/shard_map/psum | solution.py:145
  700.2 62.2 %all-reduce.4 = (f32[1024]{0:T(1024)}, f32[4,1024]{1,0:T(4,128)}, f32[4,256]{1,0:T(4,128)}, f32[16]{0:T(128)}, f32[16]{0:T(128)}, /*index=5*/f32[16]{0:T(128)}, f32[1024]{0:T(1024)}) all-reduce(f32[1024]{0:T(1024)S(1)} %get-tuple-element.317, f32[4,1024]{1,0:T(4,128)S(1)} %slice.219, ...), channel_id=1, replica_groups=mesh['fsdp'=4,'ctx'=4,'tp'=2] {'fsdp','ctx'}, use_global_device_ids=true, to_apply=%region_27.28 | all-reduce | flops 7216 | bytes 57728 | tf_op jit(solution)/shard_map/psum | solution.py:254
  765.2 7.0 all_gather.60
  (327 shorter events, 162.7 us)
Async XLA Ops:
  7.2 59.4 %all-gather.13.cloned.1.call-start = ((), (), s32[]{:S(2)}) async-start(), calls=%async_computation.10 | async-start | bytes 2621440 | tf_op jit(solution)/shard_map/all_gather | solution.py:93
  7.9 96.3 %all-gather.25.cloned.1.call-start = ((), (), s32[]{:S(2)}) async-start(), calls=%async_computation.24 | async-start | bytes 2621440 | tf_op jit(solution)/shard_map/all_gather | solution.py:20
  69.0 2.6 collective-permute-start
  80.2 71.5 %all-gather.15.cloned.1.call-start = ((), (), s32[]{:S(2)}) async-start(), calls=%async_computation.11 | async-start | bytes 2621440 | tf_op jit(solution)/shard_map/all_gather | solution.py:92
  80.9 117.2 %all-gather.17.cloned.1.call-start = ((), (), s32[]{:S(2)}) async-start(), calls=%async_computation.12 | async-start | bytes 2621440 | tf_op jit(solution)/shard_map/all_gather | solution.py:96
  81.5 162.7 %all-gather.27.cloned.1.call-start = ((), (), s32[]{:S(2)}) async-start(), calls=%async_computation.25 | async-start | bytes 2621440 | tf_op jit(solution)/shard_map/all_gather | solution.py:20
  218.3 99.9 %reduce-scatter.15.cloned.1.call-start = ((), (), s32[]{:S(2)}) async-start(), calls=%async_computation.13 | async-start | bytes 5242880 | tf_op jit(solution)/shard_map/reduce_scatter | solution.py:234
  224.3 173.7 %reduce-scatter.29.cloned.1.call-start = ((), (), s32[]{:S(2)}) async-start(), calls=%async_computation.22 | async-start | bytes 5242880 | tf_op jit(solution)/shard_map/reduce_scatter | solution.py:238
  228.3 249.2 %reduce-scatter.19.cloned.1.call-start = ((), (), s32[]{:S(2)}) async-start(), calls=%async_computation.16 | async-start | bytes 5242880 | tf_op jit(solution)/shard_map/reduce_scatter | solution.py:235
  280.9 3.1 collective-permute-start.1
  289.5 210.4 %reduce-scatter.27.cloned.1.call-start = ((), (), s32[]{:S(2)}) async-start(), calls=%async_computation.21 | async-start | bytes 81920 | tf_op jit(solution)/shard_map/reduce_scatter | solution.py:237
  300.3 227.8 %reduce-scatter.23.cloned.1.call-start = ((), (), s32[]{:S(2)}) async-start(), calls=%async_computation.19 | async-start | bytes 1310720 | tf_op jit(solution)/shard_map/reduce_scatter | solution.py:236
  314.8 239.6 %reduce-scatter.17.cloned.1.call-start = ((), (), s32[]{:S(2)}) async-start(), calls=%async_computation.14 | async-start | bytes 1310720 | tf_op jit(solution)/shard_map/reduce_scatter | solution.py:241
  318.3 263.3 %reduce-scatter.33.cloned.1.call-start = ((), (), s32[]{:S(2)}) async-start(), calls=%async_computation.27 | async-start | bytes 1310720
  400.5 208.7 %reduce-scatter.21.cloned.1.call-start = ((), (), s32[]{:S(2)}) async-start(), calls=%async_computation.17 | async-start | bytes 1310720 | tf_op jit(solution)/shard_map/reduce_scatter | solution.py:242
  477.5 154.1 %reduce-scatter.31.cloned.1.call-start = ((), (), s32[]{:S(2)}) async-start(), calls=%async_computation.26 | async-start | bytes 163840
  501.5 196.8 %all-reduce.10.cloned.1.call-start = ((), (), s32[]{:S(2)}) async-start(), calls=%async_computation.28 | async-start | bytes 4194304 | tf_op jit(solution)/shard_map/psum | solution.py:145
  502.8 106.7 %copy-start.53 = (f32[1,1280]{1,0:T(1,128)S(1)}, f32[1,1280]{1,0:T(1,128)}, u32[]{:S(2)}) copy-start(f32[1,1280]{1,0:T(1,128)} %copy-done.52) | copy-start | bytes 15364
  502.8 106.7 %copy-start.55 = (f32[1,1280]{1,0:T(1,128)S(1)}, f32[1,1280]{1,0:T(1,128)}, u32[]{:S(2)}) copy-start(f32[1,1280]{1,0:T(1,128)} %copy-done.54) | copy-start | bytes 15364
  502.8 195.5 %copy-start.27 = (bf16[1024,256]{1,0:T(8,128)(2,1)S(1)}, bf16[1024,256]{1,0:T(8,128)(2,1)}, u32[]{:S(2)}) copy-start(bf16[1024,256]{1,0:T(8,128)(2,1)} %copy-done.26) | copy-start | bytes 1572868
  502.8 262.4 %reduce-scatter.25.cloned.1.call-start = ((), (), s32[]{:S(2)}) async-start(), calls=%async_computation.20 | async-start | bytes 327680 | tf_op jit(solution)/shard_map/reduce_scatter | solution.py:243
  528.1 244.2 %all-gather.19.cloned.1.call-start = ((), (), s32[]{:S(2)}) async-start(), calls=%async_computation.15 | async-start | bytes 1310720 | tf_op jit(solution)/shard_map/all_gather | solution.py:248
  554.4 217.9 %all-gather.23.cloned.1.call-start = ((), (), s32[]{:S(2)}) async-start(), calls=%async_computation.23 | async-start | bytes 1310720 | tf_op jit(solution)/shard_map/all_gather | solution.py:252
  581.6 194.9 %all-gather.21.cloned.1.call-start = ((), (), s32[]{:S(2)}) async-start(), calls=%async_computation.18 | async-start | bytes 1310720 | tf_op jit(solution)/shard_map/all_gather | solution.py:249
  (74 other events, 1105.1 us)
Sparse Core Ops, SparseCore 0:
  9.6 56.9 all-gather.12
  80.3 23.7 all-gather.24
  105.7 45.9 all-gather.14
  153.1 44.9 all-gather.16
  218.4 20.8 all-gather.26
  241.5 76.7 reduce-scatter.14
  320.6 77.2 reduce-scatter.28
  400.2 77.2 reduce-scatter.18
  480.4 19.4 reduce-scatter.26
  502.7 25.3 reduce-scatter.22
  530.8 23.5 reduce-scatter.16
  556.7 24.8 reduce-scatter.32
  584.3 24.8 reduce-scatter.20
  612.1 19.5 reduce-scatter.30
  635.2 63.0 all-reduce.9
  700.6 20.0 reduce-scatter.24
  722.2 16.9 all-gather.18
  740.6 16.7 all-gather.22
  759.1 17.4 all-gather.20
where the time goes:
time: 796 us; the launch traced here: 787 us
  waiting for transfers between devices  466 us (59%)
  blocking collectives  142 us (18%)
  matrix products  71.4 us (9%)
  local copies, waits for them, and re-layouts  50.8 us (6%)
  other arithmetic  36.6 us (5%)
  between operations  15.3 us (2%)
    reduce_scatter x1, waiting for transfers between devices, on_device(): lax.psum_scatter(weight_grads[4], 'fsdp', scatter_dimension=1, tiled=True)  79.6 us
    reduce_scatter x1, waiting for transfers between devices, on_device(): lax.psum_scatter(weight_grads[1], 'fsdp', scatter_dimension=0, tiled=True)  77 us
    psum x1, blocking collectives, on_device(): lax.psum((grad_input_gain, grad_taps[:, :inner_here], grad_bc_conv, grad_...  62.2 us
    psum x1, waiting for transfers between devices, on_device(): lax.psum(jnp.dot(normed_out, full_out, preferred_element_type=jnp.float32...  59.9 us
    unnamed x21, waiting for transfers between devices  51.5 us
    all_gather x1, waiting for transfers between devices, on_device(): lax.all_gather(out_proj, 'fsdp', axis=1, tiled=True)  37.8 us
    all_gather x1, waiting for transfers between devices, on_device(): lax.all_gather(gate_proj, 'fsdp', axis=0, tiled=True)  36.8 us
    reduce_scatter x1, waiting for transfers between devices, on_device(): lax.psum_scatter(sectioned[1], 'ctx', scatter_dimension=0, tiled=True)  27.6 us
  transfers between devices with their start and end apart: 21, of which 17 were waited for; matrix products, arithmetic and copies ran while one was open for 16% of the time, Pallas kernels for 0%

commit v1 on v0

--- a/solution.py
+++ b/solution.py
@@ -1,3 +1,4 @@
+import functools
 import jax
 import jax.numpy as jnp
 from jax import lax
@@ -5,6 +6,35 @@
 
 EPSILON = 1e-05
 FINE = lax.Precision.HIGHEST
+
+
+def sources_all_settle(a0, axis_key):
+    runs = []
+    arr_out, item_now, moved = (lax.axis_size(axis_key), lax.axis_index(axis_key), a0.shape[0])
+    for pp, k in enumerate(a0.shape):
+        runs.append(k * arr_out if pp == 0 else k)
+    a_now = lax.dynamic_update_slice_in_dim(jnp.zeros(runs, a0.dtype), a0, item_now * moved, axis=0)
+    right_arr = wide_out = a0
+    for dd in range(1, arr_out // 2 + 1):
+        table = []
+        for pp in range(arr_out):
+            table.append((pp, (pp + 1) % arr_out))
+        right_arr = lax.ppermute(right_arr, axis_name=axis_key, perm=table)
+        a_now = lax.dynamic_update_slice_in_dim(
+            a_now, right_arr, (item_now - dd) % arr_out * moved, axis=0
+        )
+        if 2 * dd < arr_out:
+            stack_in = []
+            for pp in range(arr_out):
+                stack_in.append((pp, (pp - 1) % arr_out))
+            wide_out = lax.ppermute(wide_out, axis_name=axis_key, perm=stack_in)
+            a_now = lax.dynamic_update_slice_in_dim(
+                a_now, wide_out, (item_now + dd) % arr_out * moved, axis=0
+            )
+    return a_now
+
+
+begin_loads = functools.partial(sources_all_settle, axis_key="fsdp")
 
 
 def from_behind(block, axis, distance):
@@ -91,7 +121,7 @@
     full_gate, full_x, full_bc, full_dt, full_out = (
         lax.all_gather(gate_proj, "fsdp", axis=0, tiled=True),
         lax.all_gather(x_proj, "fsdp", axis=0, tiled=True),
-        lax.all_gather(bc_proj, "fsdp", axis=0, tiled=True),
+        begin_loads(bc_proj),
         lax.all_gather(dt_proj, "fsdp", axis=0, tiled=True),
         lax.all_gather(out_proj, "fsdp", axis=1, tiled=True),
     )

time: 796 us -> 792 us (level)
  blocking collectives: 142 us -> 118 us
  waiting for transfers between devices: 466 us -> 479 us
    all_gather x1 -> x0, blocking collectives: 22.7 us -> none  [on_device(): lax.all_gather(bc_proj, 'fsdp', axis=0, tiled=True)]
    ppermute x0 -> x3, waiting for transfers between devices: none -> 9.59 us  [the longest x2 9.59 us: sources_all_settle(): right_arr = lax.ppermute(right_arr, axis_name=axis_key, perm=table)]
    unnamed x163 -> x153, local copies, waits for them, and re-layouts: 18.6 us -> 18.1 us
  transfers between devices with their start and end apart: 21 -> 24, of which waited for: 17 -> 17; matrix products, arithmetic and copies ran while one was open for 16% -> 16% of each run, Pallas kernels for 0% -> 0%
where the time goes in v1:
time: 792 us; the launch traced here: 782 us
  waiting for transfers between devices  479 us (60%)
  blocking collectives  118 us (15%)
  matrix products  71.2 us (9%)
  local copies, waits for them, and re-layouts  52.9 us (7%)
  other arithmetic  36 us (5%)
  between operations  15.4 us (2%)
  starting transfers between devices  9.64 us (1%)
    reduce_scatter x1, waiting for transfers between devices, on_device(): lax.psum_scatter(weight_grads[4], 'fsdp', scatter_dimension=1, tiled=True)  79.6 us
    reduce_scatter x1, waiting for transfers between devices, on_device(): lax.psum_scatter(weight_grads[1], 'fsdp', scatter_dimension=0, tiled=True)  77 us
    psum x1, blocking collectives, on_device(): lax.psum((grad_input_gain, grad_taps[:, :inner_here], grad_bc_conv, grad_...  62.2 us
    psum x1, waiting for transfers between devices, on_device(): lax.psum(jnp.dot(normed_out, full_out, preferred_element_type=jnp.float32...  59.9 us
    unnamed x21, waiting for transfers between devices  51.6 us
    all_gather x1, waiting for transfers between devices, on_device(): lax.all_gather(out_proj, 'fsdp', axis=1, tiled=True)  37.7 us
    all_gather x1, waiting for transfers between devices, on_device(): lax.all_gather(gate_proj, 'fsdp', axis=0, tiled=True)  36.8 us
    reduce_scatter x1, waiting for transfers between devices, on_device(): lax.psum_scatter(sectioned[1], 'ctx', scatter_dimension=0, tiled=True)  27.5 us
  transfers between devices with their start and end apart: 24, of which 17 were waited for; matrix products, arithmetic and copies ran while one was open for 16% of the time, Pallas kernels for 0%

profile of v1, /device:TPU:0, one launch (start us, length us, event | category | flops | bytes accessed | tf_op | source)
XLA Modules:
  0.0 782.2 jit_solution(17402102279306774143)
XLA Ops:
  13.1 13.8 %all_gather.46 = bf16[1024,16]{0,1:T(8,128)(2,1)S(1)} all-gather(bf16[256,16]{0,1:T(8,128)(2,1)} %param.31), channel_id=1, replica_groups=mesh['fsdp'=4,'ctx'=4,'tp'=2] {'fsdp'}, dimensions={0}, use_global_device_ids=true | all-gather | bytes 40960 | tf_op jit(solution)/shard_map/all_gather | solution.py:125
  33.4 9.6 %collective-permute-done.2 = bf16[256,256]{1,0:T(8,128)(2,1)S(1)} collective-permute-done((bf16[256,256]{1,0:T(8,128)(2,1)S(1)}, bf16[256,256]{1,0:T(8,128)(2,1)S(1)}, u32[]{:S(2)}, u32[]{:S(2)}) %collective-permute-start.2) | collective-permute-done | bytes 131104 | tf_op jit(solution)/shard_map/ppermute | solution.py:22
  43.5 17.7 %all-gather.13.cloned.1.call-done = bf16[1024,1024]{1,0:T(8,128)(2,1)} async-done(((bf16[256,1024]{1,0:T(8,128)(2,1)}), bf16[1024,1024]{1,0:T(8,128)(2,1)}) %all-gather.13.cloned.1.call-update) | async-done | bytes 2097168 | tf_op jit(solution)/shard_map/all_gather | solution.py:123
  79.0 6.2 all-gather
  91.7 8.0 %all-gather.25.cloned.1.call-done = f32[64,64,128]{2,1,0:T(8,128)} async-done(((f32[16,64,128]{2,1,0:T(8,128)}), f32[64,64,128]{2,1,0:T(8,128)}) %all-gather.25.cloned.1.call-update) | async-done | bytes 2097168 | tf_op jit(solution)/shard_map/all_gather | solution.py:50
  101.8 6.0 fusion.36
  110.4 36.8 %all-gather.15.cloned.1.call-done = bf16[1024,1024]{1,0:T(8,128)(2,1)} async-done(((bf16[256,1024]{1,0:T(8,128)(2,1)}), bf16[1024,1024]{1,0:T(8,128)(2,1)}) %all-gather.15.cloned.1.call-update) | async-done | bytes 2097168 | tf_op jit(solution)/shard_map/all_gather | solution.py:122
  155.8 37.7 %all-gather.17.cloned.1.call-done = bf16[1024,1024]{1,0:T(8,128)(2,1)} async-done(((bf16[1024,256]{1,0:T(8,128)(2,1)}), bf16[1024,1024]{1,0:T(8,128)(2,1)}) %all-gather.17.cloned.1.call-update) | async-done | bytes 2097168 | tf_op jit(solution)/shard_map/all_gather | solution.py:126
  197.6 5.5 psum.93
  226.5 8.6 %fusion.8 = (f32[16,256]{1,0:T(8,128)}, f32[16,256]{1,0:T(8,128)}, f32[16,256]{1,0:T(8,128)}, f32[256,256]{1,0:T(8,128)S(1)}) fusion(f32[16,256]{1,0:T(8,128)S(1)} %copy-done.50, f32[256,256]{1,0:T(8,128)} %fusion.92, f32[16,256]{1,0:T(8,128)} %bitcast_add_fusion.8, pred[256,256]{1,0:T(8,128)(4,1)} %iota_compare_fusion, f32[16,64,256]{2,1,0:T(8,128)} %bitcast.308, ...), kind=kOutput, calls=%fused_computation.20 | convolution fusion | flops 820957184 | bytes 2768896 | tf_op jit(solution)/shard_map/transpose(jvp(bhts,bshp->bthp))/dot_general | solution.py:79
  239.8 6.0 while.31
  296.9 12.9 %all-reduce.11 = (bf16[256,256]{1,0:T(8,128)(2,1)S(1)}, f32[4,256]{1,0:T(4,128)}) all-reduce(f32[256,256]{1,0:T(8,128)S(1)} %slice_bitcast_fusion, f32[4,256]{1,0:T(4,128)S(1)} %pad_maximum_fusion.2), channel_id=1, replica_groups=mesh['fsdp'=4,'ctx'=4,'tp'=2] {'tp'}, use_global_device_ids=true, to_apply=%region_24.25 | all-reduce | flops 66560 | bytes 401408 | tf_op jit(solution)/shard_map/psum | solution.py:229
  313.8 79.6 %reduce-scatter.29.cloned.1.call-done = f32[1024,256]{1,0:T(8,128)} async-done(((f32[1024,1024]{1,0:T(8,128)}), f32[1024,256]{1,0:T(8,128)}) %reduce-scatter.29.cloned.1.call-update) | async-done | bytes 1048592 | tf_op jit(solution)/shard_map/reduce_scatter | solution.py:268
  396.1 77.0 %reduce-scatter.19.cloned.1.call-done = f32[256,1024]{1,0:T(8,128)} async-done(((f32[1024,1024]{1,0:T(8,128)}), f32[256,1024]{1,0:T(8,128)}) %reduce-scatter.19.cloned.1.call-update) | async-done | bytes 1048592 | tf_op jit(solution)/shard_map/reduce_scatter | solution.py:265
  479.4 16.1 %reduce-scatter.27.cloned.1.call-done = f32[256,16]{0,1:T(8,128)} async-done(((f32[1024,16]{0,1:T(8,128)}), f32[256,16]{0,1:T(8,128)}) %reduce-scatter.27.cloned.1.call-update) | async-done | bytes 16400 | tf_op jit(solution)/shard_map/reduce_scatter | solution.py:267
  498.4 25.3 %reduce-scatter.23.cloned.1.call-done = f32[256,256]{1,0:T(8,128)} async-done(((f32[1024,256]{1,0:T(8,128)}), f32[256,256]{1,0:T(8,128)}) %reduce-scatter.23.cloned.1.call-update) | async-done | bytes 262160 | tf_op jit(solution)/shard_map/reduce_scatter | solution.py:266
  523.7 26.2 %reduce-scatter.17.cloned.1.call-done = f32[64,1024]{1,0:T(8,128)} async-done(((f32[256,1024]{1,0:T(8,128)}), f32[64,1024]{1,0:T(8,128)}) %reduce-scatter.17.cloned.1.call-update) | async-done | bytes 262160 | tf_op jit(solution)/shard_map/reduce_scatter | solution.py:271
  550.0 27.2 %reduce-scatter.33.cloned.1.call-done = f32[64,1024]{1,0:T(8,128)} async-done(((f32[256,1024]{1,0:T(8,128)}), f32[64,1024]{1,0:T(8,128)}) %reduce-scatter.33.cloned.1.call-update) | async-done | bytes 262160
  577.3 27.5 %reduce-scatter.21.cloned.1.call-done = f32[64,1024]{1,0:T(8,128)} async-done(((f32[256,1024]{1,0:T(8,128)}), f32[64,1024]{1,0:T(8,128)}) %reduce-scatter.21.cloned.1.call-update) | async-done | bytes 262160 | tf_op jit(solution)/shard_map/reduce_scatter | solution.py:272
  605.0 22.2 %reduce-scatter.31.cloned.1.call-done = f32[64,16]{1,0:T(8,128)} async-done(((f32[256,16]{1,0:T(8,128)}), f32[64,16]{1,0:T(8,128)}) %reduce-scatter.31.cloned.1.call-update) | async-done | bytes 4112
  628.1 5.2 all-gather.3
  634.0 59.9 %all-reduce.10.cloned.1.call-done = (f32[1,256,1024]{2,1,0:T(8,128)}, f32[256,1024]{1,0:T(8,128)}) async-done(((f32[1,256,1024]{2,1,0:T(8,128)}, f32[256,1024]{1,0:T(8,128)}), (f32[1,256,1024]{2,1,0:T(8,128)}, f32[256,1024]{1,0:T(8,128)})) %all-reduce.10.cloned.1.call-update) | async-done | bytes 2097168 | tf_op jit(solution)/shard_map/psum | solution.py:175
  695.8 62.2 %all-reduce.4 = (f32[1024]{0:T(1024)}, f32[4,1024]{1,0:T(4,128)}, f32[4,256]{1,0:T(4,128)}, f32[16]{0:T(128)}, f32[16]{0:T(128)}, /*index=5*/f32[16]{0:T(128)}, f32[1024]{0:T(1024)}) all-reduce(f32[1024]{0:T(1024)S(1)} %get-tuple-element.317, f32[4,1024]{1,0:T(4,128)S(1)} %slice.219, ...), channel_id=1, replica_groups=mesh['fsdp'=4,'ctx'=4,'tp'=2] {'fsdp','ctx'}, use_global_device_ids=true, to_apply=%region_27.28 | all-reduce | flops 7216 | bytes 57728 | tf_op jit(solution)/shard_map/psum | solution.py:284
  760.9 7.1 all_gather.56
  (327 shorter events, 168.1 us)
Async XLA Ops:
  7.2 54.0 %all-gather.13.cloned.1.call-start = ((), (), s32[]{:S(2)}) async-start(), calls=%async_computation.10 | async-start | bytes 2621440 | tf_op jit(solution)/shard_map/all_gather | solution.py:123
  7.9 91.7 %all-gather.25.cloned.1.call-start = ((), (), s32[]{:S(2)}) async-start(), calls=%async_computation.24 | async-start | bytes 2621440 | tf_op jit(solution)/shard_map/all_gather | solution.py:50
  8.0 25.3 %collective-permute-start = (bf16[256,256]{1,0:T(8,128)(2,1)}, bf16[256,256]{1,0:T(8,128)(2,1)S(1)}, u32[]{:S(2)}, u32[]{:S(2)}) collective-permute-start(bf16[256,256]{1,0:T(8,128)(2,1)} %param.30), channel_id=1, source_target_pairs={{0,8},{8,16},{16,24},{24,0},{1,9},{9,17},{17,25},{25,1},{2,10},{10... | collective-permute-start | bytes 393224 | tf_op jit(solution)/shard_map/ppermute | solution.py:22
  11.0 22.4 %collective-permute-start.1 = (bf16[256,256]{1,0:T(8,128)(2,1)}, bf16[256,256]{1,0:T(8,128)(2,1)S(1)}, u32[]{:S(2)}, u32[]{:S(2)}) collective-permute-start(bf16[256,256]{1,0:T(8,128)(2,1)} %param.30), channel_id=1, source_target_pairs={{0,24},{8,0},{16,8},{24,16},{1,25},{9,1},{17,9},{25,17},{2,26},{10... | collective-permute-start | bytes 393224 | tf_op jit(solution)/shard_map/ppermute | solution.py:30
  33.3 9.7 %collective-permute-start.2 = (bf16[256,256]{1,0:T(8,128)(2,1)S(1)}, bf16[256,256]{1,0:T(8,128)(2,1)S(1)}, u32[]{:S(2)}, u32[]{:S(2)}) collective-permute-start(bf16[256,256]{1,0:T(8,128)(2,1)S(1)} %collective-permute-done), channel_id=1, source_target_pairs={{0,8},{8,16},{16,24},{24,0},{1,9},{9,17},{17,25},{25,1},{2,10},{10... | collective-permute-start | bytes 393224 | tf_op jit(solution)/shard_map/ppermute | solution.py:22
  63.6 3.4 collective-permute-start.3
  76.2 71.0 %all-gather.15.cloned.1.call-start = ((), (), s32[]{:S(2)}) async-start(), calls=%async_computation.11 | async-start | bytes 2621440 | tf_op jit(solution)/shard_map/all_gather | solution.py:122
  77.0 116.6 %all-gather.17.cloned.1.call-start = ((), (), s32[]{:S(2)}) async-start(), calls=%async_computation.12 | async-start | bytes 2621440 | tf_op jit(solution)/shard_map/all_gather | solution.py:126
  77.5 162.2 %all-gather.27.cloned.1.call-start = ((), (), s32[]{:S(2)}) async-start(), calls=%async_computation.25 | async-start | bytes 2621440 | tf_op jit(solution)/shard_map/all_gather | solution.py:50
  213.8 99.9 %reduce-scatter.15.cloned.1.call-start = ((), (), s32[]{:S(2)}) async-start(), calls=%async_computation.13 | async-start | bytes 5242880 | tf_op jit(solution)/shard_map/reduce_scatter | solution.py:264
  219.8 173.7 %reduce-scatter.29.cloned.1.call-start = ((), (), s32[]{:S(2)}) async-start(), calls=%async_computation.22 | async-start | bytes 5242880 | tf_op jit(solution)/shard_map/reduce_scatter | solution.py:268
  223.8 249.3 %reduce-scatter.19.cloned.1.call-start = ((), (), s32[]{:S(2)}) async-start(), calls=%async_computation.16 | async-start | bytes 5242880 | tf_op jit(solution)/shard_map/reduce_scatter | solution.py:265
  276.5 3.1 collective-permute-start.4
  285.1 210.4 %reduce-scatter.27.cloned.1.call-start = ((), (), s32[]{:S(2)}) async-start(), calls=%async_computation.21 | async-start | bytes 81920 | tf_op jit(solution)/shard_map/reduce_scatter | solution.py:267
  295.8 227.8 %reduce-scatter.23.cloned.1.call-start = ((), (), s32[]{:S(2)}) async-start(), calls=%async_computation.19 | async-start | bytes 1310720 | tf_op jit(solution)/shard_map/reduce_scatter | solution.py:266
  311.2 238.6 %reduce-scatter.17.cloned.1.call-start = ((), (), s32[]{:S(2)}) async-start(), calls=%async_computation.14 | async-start | bytes 1310720 | tf_op jit(solution)/shard_map/reduce_scatter | solution.py:271
  313.8 263.4 %reduce-scatter.33.cloned.1.call-start = ((), (), s32[]{:S(2)}) async-start(), calls=%async_computation.27 | async-start | bytes 1310720
  396.1 208.7 %reduce-scatter.21.cloned.1.call-start = ((), (), s32[]{:S(2)}) async-start(), calls=%async_computation.17 | async-start | bytes 1310720 | tf_op jit(solution)/shard_map/reduce_scatter | solution.py:272
  473.1 154.1 %reduce-scatter.31.cloned.1.call-start = ((), (), s32[]{:S(2)}) async-start(), calls=%async_computation.26 | async-start | bytes 163840
  497.0 196.9 %all-reduce.10.cloned.1.call-start = ((), (), s32[]{:S(2)}) async-start(), calls=%async_computation.28 | async-start | bytes 4194304 | tf_op jit(solution)/shard_map/psum | solution.py:175
  498.3 262.6 %reduce-scatter.25.cloned.1.call-start = ((), (), s32[]{:S(2)}) async-start(), calls=%async_computation.20 | async-start | bytes 327680 | tf_op jit(solution)/shard_map/reduce_scatter | solution.py:273
  523.6 244.3 %all-gather.19.cloned.1.call-start = ((), (), s32[]{:S(2)}) async-start(), calls=%async_computation.15 | async-start | bytes 1310720 | tf_op jit(solution)/shard_map/all_gather | solution.py:278
  549.9 218.0 %all-gather.23.cloned.1.call-start = ((), (), s32[]{:S(2)}) async-start(), calls=%async_computation.23 | async-start | bytes 1310720 | tf_op jit(solution)/shard_map/all_gather | solution.py:282
  577.2 194.9 %all-gather.21.cloned.1.call-start = ((), (), s32[]{:S(2)}) async-start(), calls=%async_computation.18 | async-start | bytes 1310720 | tf_op jit(solution)/shard_map/all_gather | solution.py:279
  (72 other events, 1373.3 us)
Sparse Core Ops, SparseCore 0:
  9.6 51.5 all-gather.12
  76.4 23.2 all-gather.24
  101.2 45.9 all-gather.14
  148.6 44.8 all-gather.16
  214.0 20.8 all-gather.26
  237.0 76.7 reduce-scatter.14
  316.2 77.2 reduce-scatter.28
  395.8 77.2 reduce-scatter.18
  476.0 19.4 reduce-scatter.26
  498.2 25.3 reduce-scatter.22
  526.3 23.5 reduce-scatter.16
  552.3 24.8 reduce-scatter.32
  579.9 24.8 reduce-scatter.20
  607.6 19.5 reduce-scatter.30
  630.7 63.0 all-reduce.9
  696.2 20.0 reduce-scatter.24
  717.8 16.9 all-gather.18
  736.2 16.7 all-gather.22
  754.7 17.4 all-gather.20
